TPU v7x, 32 devices: a whole 2x2x4 slice. The times are simulated.
32 devices in a mesh: seq: 8 (over z, x), rep: 4 (over y, core).
Axes of the slice: x: 2, y: 2, z: 4, core: 2. Of those that a mesh axis runs over, the one named last changes fastest.
Arguments:
- states: bfloat16 [6144, 512], P(('rep', 'seq')), parts along dimension 0, may hold values from -6 to 6
- starts: int32 [1024], P(('rep', 'seq')), parts along dimension 0, may hold values from 0 to 1535, as said below
- straddle: int32 [32], P(('rep', 'seq')), parts along dimension 0, may hold values from 0 to 63, as said below
- key_weight: bfloat16 [512, 512], replicated
- out_weight: bfloat16 [512, 4096], P(None, 'seq'), may hold values from -0.25 to 0.25
- norm_gain: bfloat16 [4096], P('seq'), may hold values from 0.25 to 1.75
- attn_weight: bfloat16 [4096, 3, 4096], P(None, None, 'seq')
Outputs:
- attended: bfloat16 [1024, 4096], P(('rep', 'seq')), parts along dimension 0
There are 4 independent parts, one for each index of `rep`. A program takes and returns all parts, laid end to end along the dimension named above; an argument that names none is the same for every part. Nothing has to cross between parts.
Inputs may be any that keep to these rules, and one draw needn't show every extreme that they name: Rising; shard s of 192 bytes holds the starts of exactly 32 patches, numbers s * 32 to (s+1) * 32 - 1; the first of them lies at most 63 bytes into the shard, and at byte 0 for shard 0. `straddle`: entry s equals the first start of shard s+1 minus (s+1) * 192; the last entry is 0.
All inputs are finite; a program needn't handle non-finite values.
Results may differ from a plain program's by a relative error of at most 0.0096.
Values may be sent and summed in bfloat16 or wider, within the bound.
A program may use at most 64 MiB of HBM per device.

v0:
```python
import jax
import jax.numpy as jnp
from jax import lax
from jax.sharding import PartitionSpec as P

HD = 128
LHD = 128
HALO = 64


epsilon = 1e-05


def shifted(shard, axis, by):
    size = lax.axis_size(axis)
    pairs = [(i, i + by) for i in range(size) if 0 <= i + by < size]
    return lax.ppermute(shard, axis, pairs)


def cross_pool(window, local_starts, halo_count, key_weight, patch_total, head_size):
    window_rows = window.shape[0]
    shard_bytes = window_rows - HALO
    width = window.shape[1]
    head_count = width // head_size
    position = jnp.arange(window_rows, dtype=jnp.int32)
    patch_ends = jnp.concatenate([local_starts[1:], (shard_bytes + halo_count).reshape(1)])
    member = (position[None, :] >= local_starts[:, None]) & (
        position[None, :] < patch_ends[:, None]
    )
    byte_count = jnp.sum(member.astype(jnp.float32), axis=1)
    query = (
        jnp.dot(member.astype(jnp.bfloat16), window, preferred_element_type=jnp.float32)
        / byte_count[:, None]
    ).astype(jnp.bfloat16)
    keys = jnp.dot(window, key_weight, preferred_element_type=jnp.float32).astype(jnp.bfloat16)
    query_heads = query.reshape(patch_total, head_count, head_size)
    key_heads = keys.reshape(window_rows, head_count, head_size)
    scores = jnp.einsum(
        "phd,jhd->hpj", query_heads, key_heads, preferred_element_type=jnp.float32
    ) / jnp.sqrt(jnp.float32(head_size))
    scores = jnp.where(member[None], scores, jnp.float32(-1e30))
    row_peak = jnp.max(scores, axis=-1, keepdims=True)
    expo = jnp.where(member[None], jnp.exp(scores - row_peak), jnp.float32(0.0))
    cross = (expo / jnp.sum(expo, axis=-1, keepdims=True)).astype(jnp.bfloat16)
    value_heads = window.reshape(window_rows, head_count, head_size)
    pooled = jnp.einsum("hpj,jhd->phd", cross, value_heads, preferred_element_type=jnp.float32)
    return pooled.reshape(patch_total, width).astype(jnp.bfloat16)


def global_attend(head_view):
    patch_count = head_view.shape[0]
    scores = jnp.einsum(
        "qhd,khd->hqk", head_view[:, 0], head_view[:, 1], preferred_element_type=jnp.float32
    ) / jnp.sqrt(jnp.float32(HD))
    causal = jnp.arange(patch_count)[:, None] >= jnp.arange(patch_count)[None, :]
    scores = jnp.where(causal[None], scores, jnp.float32(-1e30))
    row_peak = jnp.max(scores, axis=-1, keepdims=True)
    expo = jnp.where(causal[None], jnp.exp(scores - row_peak), jnp.float32(0.0))
    probs = (expo / jnp.sum(expo, axis=-1, keepdims=True)).astype(jnp.bfloat16)
    attended = jnp.einsum(
        "hqk,khd->qhd", probs, head_view[:, 2], preferred_element_type=jnp.float32
    )
    return attended.reshape(patch_count, head_view.shape[2] * HD).astype(jnp.bfloat16)


def norm_rows(embedding, gain_row):
    meansq = jnp.mean(embedding * embedding, axis=1, keepdims=True)
    return (embedding * lax.rsqrt(meansq + epsilon) * gain_row.astype(jnp.float32)).astype(
        jnp.bfloat16
    )


def shards(states, starts, straddle, key_weight, out_weight, norm_gain, attn_weight):
    shard_index = lax.axis_index("seq")
    byte_rows = states.shape[0]
    patch_local = starts.shape[0]
    halo_rows = shifted(states[:HALO], "seq", -1)
    window = jnp.concatenate([states, halo_rows], axis=0)
    local_starts = starts - shard_index * byte_rows
    pooled = cross_pool(window, local_starts, straddle[0], key_weight, patch_local, LHD)
    local_width = attn_weight.shape[2]
    model_width = attn_weight.shape[0]
    proj_weight = attn_weight.reshape(model_width, 3 * local_width)
    pooled_every = lax.all_gather(pooled, "seq", axis=0, tiled=True)
    out_whole, gain_whole = (
        lax.all_gather(out_weight, "seq", axis=1, tiled=True),
        lax.all_gather(norm_gain.reshape(1, -1), "seq", axis=1, tiled=True),
    )
    embedding = jnp.dot(pooled_every, out_whole, preferred_element_type=jnp.float32)
    normed = norm_rows(embedding, gain_whole)
    projected = jnp.dot(normed, proj_weight, preferred_element_type=jnp.float32).astype(
        jnp.bfloat16
    )
    head_view = projected.reshape(projected.shape[0], 3, local_width // HD, HD)
    attended = global_attend(head_view)
    return lax.all_to_all(attended, "seq", split_axis=0, concat_axis=1, tiled=True)


def solution(mesh):
    placed = (
        P(("rep", "seq"), None),
        P(("rep", "seq")),
        P(("rep", "seq")),
        P(),
        P(None, "seq"),
        P("seq"),
        P(None, None, "seq"),
    )
    return jax.shard_map(
        shards, mesh=mesh, in_specs=placed, out_specs=P(("rep", "seq"), None), check_vma=False
    )
```

profile of v0, /device:TPU:0, one launch (start us, length us, event | category | flops | bytes accessed | tf_op | source)
XLA Modules:
  0.0 122.1 jit_solution(7159257700888569722)
XLA Ops:
  6.5 0.7 all-gather.4.cloned.1.call-update
  7.3 1.1 copy.41
  8.3 1.3 %collective-permute-start = (bf16[64,512]{0,1:T(8,128)(2,1)S(1)}, bf16[64,512]{0,1:T(8,128)(2,1)S(1)}, u32[]{:S(2)}, u32[]{:S(2)}) collective-permute-start(bf16[64,512]{0,1:T(8,128)(2,1)S(1)} %slice.20), channel_id=1, source_target_pairs={{4,0},{8,4},{12,8},{16,12},{20,16},{24,20},{28,24},{5,1},{9,5},{13... | collective-permute-start | bytes 196616 | tf_op jit(solution)/shard_map/ppermute | solution.py:17
  9.6 0.7 broadcast_subtract_fusion
  11.0 17.0 %copy.46 = bf16[4096,3,512]{0,2,1:T(8,128)(2,1)} copy(bf16[4096,3,512]{2,0,1:T(8,128)(2,1)} %param.13) | data formatting | bytes 25165824 | tf_op args[6]
  28.0 30.0 %all-gather.1 = bf16[8,1,512]{2,1,0:T(2,128)(2,1)S(1)} all-gather(bf16[1,1,512]{2,1,0:T(2,128)(2,1)S(1)} %reshape.102), channel_id=2, replica_groups=mesh['seq'=8,'rep'=4] {'seq'}, dimensions={0}, use_global_device_ids=true | all-gather | bytes 9216 | tf_op jit(solution)/shard_map/all_gather | solution.py:87
  58.2 0.2 convert_reduce_fusion
  58.5 0.1 pad_maximum_fusion
  58.6 0.2 fusion.16
  58.8 0.3 fusion.8
  59.2 0.4 fusion.29
  59.5 0.2 fusion.15
  59.8 31.8 %all_gather.9 = bf16[256,512]{1,0:T(8,128)(2,1)S(1)} all-gather(bf16[32,512]{1,0:T(8,128)(2,1)S(1)} %bitcast.59), channel_id=1, replica_groups=mesh['seq'=8,'rep'=4] {'seq'}, dimensions={0}, use_global_device_ids=true | all-gather | bytes 294912 | tf_op jit(solution)/shard_map/all_gather | solution.py:84
  91.6 3.5 %multiply_reduce_fusion = (f32[256]{0:T(256)S(1)}, f32[256,4096]{1,0:T(8,128)S(1)}) fusion(bf16[256,512]{1,0:T(8,128)(2,1)S(1)} %all_gather.9, bf16[512,4096]{1,0:T(8,128)(2,1)} %all-gather.4.cloned.1.call-done), kind=kOutput, calls=%fused_computation.3 | convolution fusion | flops 1075838720 | bytes 8651776 | tf_op jit(solution)/shard_map/dot_general | solution.py:89
  95.2 6.6 %convolution_convert_fusion = bf16[256,1536]{1,0:T(8,128)(2,1)S(1)} fusion(bf16[4096,1536]{0,1:T(8,128)(2,1)} %bitcast.56, f32[256,4096]{1,0:T(8,128)S(1)} %get-tuple-element.11, f32[4096]{0:T(1024)S(1)} %bitcast.60, f32[256]{0:T(256)S(1)} %add_rsqrt_fusion), kind=kOutput, calls=%fused_computation.4 | convolution fusion | flops 3224764416 | bytes 17581056 | tf_op jit(solution)/shard_map/dot_general | solution.py:91
  101.8 0.2 reshape.97
  102.0 0.3 fusion.28
  102.3 0.2 copy.55
  102.4 0.6 fusion.30
  103.0 0.2 fusion.9
  103.3 0.2 copy.51
  103.5 0.1 convert_element_type.54
  103.6 10.9 %all_to_all.16 = bf16[8,32,512]{2,1,0:T(8,128)(2,1)S(1)} all-to-all(bf16[8,32,512]{2,1,0:T(8,128)(2,1)S(1)} %convert_element_type.54), channel_id=1, replica_groups=mesh['seq'=8,'rep'=4] {'seq'}, dimensions={0} | all-to-all | bytes 524288 | tf_op jit(solution)/shard_map/all_to_all | solution.py:96
  114.5 0.7 copy.61
  (16 shorter events, 0.4 us)
Async XLA Ops:
  6.5 52.3 %copy-start = (bf16[512,512]{1,0:T(8,128)(2,1)S(1)}, bf16[512,512]{1,0:T(8,128)(2,1)}, u32[]{:S(2)}) copy-start(bf16[512,512]{1,0:T(8,128)(2,1)} %param.10) | copy-start | bytes 1572868
  6.5 85.1 %all-gather.4.cloned.1.call-start = ((), (), s32[]{:S(2)}) async-start(), calls=%async_computation.1 | async-start | bytes 4718592 | tf_op jit(solution)/shard_map/all_gather | solution.py:86
  8.3 50.1 %collective-permute-start = (bf16[64,512]{0,1:T(8,128)(2,1)S(1)}, bf16[64,512]{0,1:T(8,128)(2,1)S(1)}, u32[]{:S(2)}, u32[]{:S(2)}) collective-permute-start(bf16[64,512]{0,1:T(8,128)(2,1)S(1)} %slice.20), channel_id=1, source_target_pairs={{4,0},{8,4},{12,8},{16,12},{20,16},{24,20},{28,24},{5,1},{9,5},{13... | collective-permute-start | bytes 196616 | tf_op jit(solution)/shard_map/ppermute | solution.py:17
  11.0 17.0 %copy-start.1 = (bf16[512]{0:T(512)(128)(2,1)S(1)}, bf16[512]{0:T(512)(128)(2,1)}, u32[]{:S(2)}) copy-start(bf16[512]{0:T(512)(128)(2,1)} %param.12) | copy-start | bytes 3076
Sparse Core Ops, SparseCore 0:
  9.4 81.6 all-gather.3
where the time goes:
time: 123 us; the launch traced here: 122 us
  blocking collectives  72.8 us (59%)
  local copies, waits for them, and re-layouts  19.8 us (16%)
  between operations  14.2 us (12%)
  matrix products  12.1 us (10%)
  starting transfers between devices  1.29 us (1%)
    all_gather x1, blocking collectives, shards(): pooled_every = lax.all_gather(pooled, 'seq', axis=0, tiled=True)  31.8 us
    all_gather x1, blocking collectives, shards(): lax.all_gather(norm_gain.reshape(1, -1), 'seq', axis=1, tiled=True)  30 us
    unnamed x8, local copies, waits for them, and re-layouts  18.2 us
    all_to_all x1, blocking collectives, shards(): lax.all_to_all(attended, 'seq', split_axis=0, concat_axis=1, tiled=True)  10.9 us
    dot_general x1, matrix products, shards(): jnp.dot(normed, proj_weight, preferred_element_type=jnp.float32)  6.62 us
    dot_general x1, matrix products, shards(): jnp.dot(pooled_every, out_whole, preferred_element_type=jnp.float32)  3.54 us
  transfers between devices with their start and end apart: 2, of which 0 were waited for; matrix products, arithmetic and copies ran while one was open for 17% of the time, Pallas kernels for 0%

commit v1 on v0

v1 whole, which is shorter than its diff:
```python
import functools
import math

import jax
import jax.numpy as jnp
from jax import lax
from jax.experimental import pallas as pl
from jax.experimental.pallas import tpu as pltpu
from jax.sharding import PartitionSpec as P

HD = 128
LHD = 128
HALO = 64
CORES = 2
PAD = 16

epsilon = 1e-05

BF16 = jnp.bfloat16
F32 = jnp.float32


def dot(a, b):
    return jnp.dot(a, b, preferred_element_type=F32)


def dot_t(a, b):
    return lax.dot_general(a, b, (((1,), (1,)), ((), ())), preferred_element_type=F32)


def softmax_dot(scores, keep, values):
    scores = jnp.where(keep, scores, F32(-1e30))
    peak = jnp.max(scores, axis=-1, keepdims=True)
    expo = jnp.where(keep, jnp.exp(scores - peak), F32(0.0))
    total = jnp.sum(expo, axis=-1, keepdims=True)
    return dot((expo / total).astype(BF16), values).astype(BF16)


def kernel(
    nz, nx, ny,
    states, starts, straddle, key_weight, out_weight, gain, attn_weight,
    out,
    window, kw, ow, w, pg, acc, att,
    l_sem, w_sem, h_sem,
    zs_sem, xs_sem, m_sem, ys_sem, yr_sem, cs_sem, cr_sem,
    ps_sem, pr_sem, as_sem, ar_sem,
):
    n = nz * nx
    s = lax.axis_index("seq")
    r = lax.axis_index("rep")
    zi, xi = s // nx, s % nx
    yi, ci = r // CORES, r % CORES
    other = yi * CORES + (1 - ci)
    rows, width = states.shape
    patches = starts.shape[1]
    cols = out_weight.shape[2]
    heads = cols // HD
    model = cols * n

    def seq_of(kz, kx):
        return ((zi + nz + kz) % nz) * nx + (xi + nx + kx) % nx

    def rep_of(ky):
        return ((yi + ny + ky) % ny) * CORES + ci

    def remote(src, dst, send, recv, seq, rep):
        return pltpu.make_async_remote_copy(
            src_ref=src, dst_ref=dst, send_sem=send, recv_sem=recv,
            device_id={"seq": seq, "rep": rep}, device_id_type=pl.DeviceIdType.MESH,
        )

    barrier = pltpu.get_barrier_semaphore()

    def greet(seq, rep):
        pl.semaphore_signal(
            barrier, inc=1, device_id={"seq": seq, "rep": rep},
            device_id_type=pl.DeviceIdType.MESH,
        )

    for k in range(1, n):
        greet((s + k) % n, r)
    for k in range(1, ny):
        greet(s, rep_of(k))
    greet(s, other)

    local = [
        pltpu.make_async_copy(states, window.at[pl.ds(0, rows)], l_sem.at[0]),
        pltpu.make_async_copy(key_weight, kw, l_sem.at[1]),
        pltpu.make_async_copy(out_weight, ow.at[s], l_sem.at[2]),
    ]
    for copy in local:
        copy.start()
    w_copy = pltpu.make_async_copy(attn_weight, w, w_sem)
    w_copy.start()

    pl.semaphore_wait(barrier, n - 1 + ny - 1 + 1)

    left = (s + n - 1) % n
    halo = remote(
        states.at[pl.ds(0, HALO)], window.at[pl.ds(rows, HALO)],
        h_sem.at[0], h_sem.at[1], left, r,
    )

    @pl.when(s > 0)
    def _():
        halo.start()

    sent = []

    def go(copy):
        copy.start()
        sent.append(copy)

    mine = out_weight.at[r]
    for kx in range(1, nx):
        go(remote(mine, ow.at[s, r], xs_sem.at[0, kx], m_sem.at[0, kx], seq_of(0, kx), r))
    for kz in range(1, nz):
        go(remote(mine, ow.at[s, r], zs_sem.at[kz], m_sem.at[kz, 0], seq_of(kz, 0), r))

    @pl.when(s == n - 1)
    def _():
        window[pl.ds(rows, HALO), :] = jnp.zeros((HALO, width), BF16)

    square0 = lax.broadcasted_iota(jnp.int32, (patches, patches), 0)
    square1 = lax.broadcasted_iota(jnp.int32, (patches, patches), 1)
    first = (starts[...] - s * rows).astype(F32)
    low = jnp.sum(jnp.where(square0 == square1, first, 0.0), axis=1, keepdims=True)
    high = jnp.sum(jnp.where(square0 + 1 == square1, first, 0.0), axis=1, keepdims=True)
    line = lax.broadcasted_iota(jnp.int32, (patches, 1), 0)
    high = jnp.where(line == patches - 1, (rows + straddle[0]).astype(F32), high)
    place = lax.broadcasted_iota(jnp.int32, (patches, rows + HALO), 1).astype(F32)
    member = (place >= low) & (place < high)
    count = high - low

    local[0].wait()
    local[1].wait()

    @pl.when(s < n - 1)
    def _():
        halo.wait_recv()

    whole = window[...]
    keys = dot(whole, kw[...]).astype(BF16)
    query = (dot(member.astype(BF16), whole) / count).astype(BF16)
    scale = F32(1.0 / math.sqrt(LHD))
    for h in range(width // LHD):
        part = slice(h * LHD, (h + 1) * LHD)
        pg[s, pl.ds(0, patches), part] = softmax_dot(
            dot_t(query[:, part], keys[:, part]) * scale, member, whole[:, part]
        )
    pg[s, pl.ds(patches, PAD), pl.ds(0, cols)] = jnp.broadcast_to(gain[...], (PAD, cols))
    for k in range(1, n):
        go(remote(pg.at[s], pg.at[s], ps_sem.at[k], pr_sem.at[k], (s + k) % n, r))

    def wait_for(ref, sem):
        pltpu.make_async_copy(ref, ref, sem).wait()

    order = [(kz, kx) for kx in range(nx) for kz in range(nz)][1:]
    if nx > 1:
        order = [(0, kx) for kx in range(1, nx)] + [o for o in order if o[0] > 0]
    for kz, kx in order:
        j = seq_of(-kz, -kx)
        piece = ow.at[j, r]
        wait_for(piece, m_sem.at[kz, kx])
        for ky in range(1, ny):
            go(remote(piece, piece, ys_sem.at[ky, kz, kx], yr_sem.at[ky, kz, kx], s, rep_of(ky)))
        if kx == 0:
            for k in range(1, nx):
                go(remote(piece, piece, xs_sem.at[kz, k], m_sem.at[kz, k], seq_of(0, k), r))
        go(remote(piece, piece, cs_sem.at[0, kz, kx], cr_sem.at[0, kz, kx], s, other))

    for k in range(1, n):
        wait_for(pg.at[s], pr_sem.at[k])
    pooled = pg[:, pl.ds(0, patches), :].reshape(n * patches, width)

    def project(j, squares, fresh):
        weight = ow[j].reshape(width, cols)
        embed = dot(pooled, weight)
        squares = squares + jnp.sum(embed * embed, axis=1, keepdims=True)
        row = pg[j, pl.ds(patches, PAD), pl.ds(0, cols)][0:1, :].astype(F32)
        scaled = (embed * row).astype(BF16)
        for t in range(3):
            span = slice(t * cols, (t + 1) * cols)
            term = dot(scaled, w[t, j])
            if fresh:
                acc[:, span] = term
            else:
                acc[:, span] = acc[:, span] + term
        return squares

    def arrived(kz, kx):
        j = seq_of(-kz, -kx)
        for ky in range(ny):
            wait_for(ow.at[j, other], cr_sem.at[ky, kz, kx])
        return j

    local[2].wait()
    w_copy.wait()
    squares = project(s, jnp.zeros((n * patches, 1), F32), True)
    before = None
    for kz, kx in order:
        j = seq_of(-kz, -kx)
        for ky in range(1, ny):
            piece = ow.at[j, rep_of(-ky)]
            wait_for(piece, yr_sem.at[ky, kz, kx])
            go(remote(piece, piece, cs_sem.at[ky, kz, kx], cr_sem.at[ky, kz, kx], s, other))
        if before is not None:
            squares = project(arrived(*before), squares, False)
        before = (kz, kx)
    if before is not None:
        squares = project(arrived(*before), squares, False)

    total = n * patches
    rstd = lax.rsqrt(squares / F32(model) + epsilon)
    causal = lax.broadcasted_iota(jnp.int32, (total, total), 0) >= lax.broadcasted_iota(
        jnp.int32, (total, total), 1
    )
    scale = F32(1.0 / math.sqrt(HD))
    own = []
    for h in range(heads):
        q, k, v = (
            (acc[:, t * cols + h * HD : t * cols + (h + 1) * HD] * rstd).astype(BF16)
            for t in range(3)
        )
        att[h] = softmax_dot(dot_t(q, k) * scale, causal, v).reshape(n, patches, HD)
        span = pl.ds(pl.multiple_of(s * cols + h * HD, HD), HD)
        for k in range(1, n):
            j = (s + k) % n
            go(remote(att.at[h, j], out.at[:, span], as_sem.at[h, k], ar_sem.at[h, k], j, r))
        own.append(pltpu.make_async_copy(att.at[h, s], out.at[:, span], as_sem.at[h, 0]))
        own[-1].start()

    for copy in own:
        copy.wait()
    for h in range(heads):
        for k in range(1, n):
            span = pl.ds(pl.multiple_of(((s + n - k) % n) * cols + h * HD, HD), HD)
            wait_for(out.at[:, span], ar_sem.at[h, k])
    for copy in sent:
        copy.wait_send()

    @pl.when(s > 0)
    def _():
        halo.wait_send()


def split_seq(n):
    power = 1
    while power * power < n:
        power *= 2
    return (power, n // power) if n % power == 0 else (n, 1)


def shards(states, starts, straddle, key_weight, out_weight, norm_gain, attn_weight):
    n, reps = lax.axis_size("seq"), lax.axis_size("rep")
    nz, nx = split_seq(n)
    ny = reps // CORES
    rows, width = states.shape
    patches = starts.shape[0]
    model, three, cols = attn_weight.shape
    heads = cols // HD
    total = n * patches
    w = attn_weight.transpose(1, 0, 2).reshape(three, n, model // n, cols)
    any_space = pl.BlockSpec(memory_space=pl.ANY)
    vmem = pl.BlockSpec(memory_space=pltpu.VMEM)
    smem = pl.BlockSpec(memory_space=pltpu.SMEM)
    dma = pltpu.SemaphoreType.DMA
    flops = 2 * total * (model * three * cols + width * model)
    return pl.pallas_call(
        functools.partial(kernel, nz, nx, ny),
        out_shape=jax.ShapeDtypeStruct((patches, model), BF16),
        in_specs=[any_space, vmem, smem, any_space, any_space, vmem, any_space],
        out_specs=any_space,
        scratch_shapes=[
            pltpu.VMEM((rows + HALO, width), BF16),
            pltpu.VMEM(key_weight.shape, BF16),
            pltpu.VMEM((n, reps, width // reps, cols), BF16),
            pltpu.VMEM(w.shape, BF16),
            pltpu.VMEM((n, patches + PAD, width), BF16),
            pltpu.VMEM((total, three * cols), F32),
            pltpu.VMEM((heads, n, patches, HD), BF16),
            dma((3,)), dma, dma((2,)),
            dma((nz,)), dma((nz, nx)), dma((nz, nx)),
            dma((ny, nz, nx)), dma((ny, nz, nx)), dma((ny, nz, nx)), dma((ny, nz, nx)),
            dma((n,)), dma((n,)), dma((heads, n)), dma((heads, n)),
        ],
        compiler_params=pltpu.CompilerParams(
            collective_id=0, has_side_effects=True, vmem_limit_bytes=48 * 1024 * 1024
        ),
        cost_estimate=pl.CostEstimate(
            flops=flops, bytes_accessed=w.size * 2, transcendentals=0
        ),
    )(
        states, starts.reshape(1, patches), straddle, key_weight,
        out_weight.reshape(reps, width // reps, cols), norm_gain.reshape(1, cols), w,
    )


def solution(mesh):
    placed = (
        P(("rep", "seq"), None),
        P(("rep", "seq")),
        P(("rep", "seq")),
        P(),
        P(None, "seq"),
        P("seq"),
        P(None, None, "seq"),
    )
    return jax.shard_map(
        shards, mesh=mesh, in_specs=placed, out_specs=P(("rep", "seq"), None), check_vma=False
    )
```

time: 123 us -> 52.6 us (0.43)
  blocking collectives: 72.8 us -> 0 us
  Pallas kernels: 0 us -> 46.7 us
  local copies, waits for them, and re-layouts: 19.8 us -> 5.05 us
  between operations: 14.2 us -> 0.67 us
  matrix products: 12.1 us -> 0 us
  starting transfers between devices: 1.29 us -> 0 us
    all_gather x2 -> x0, blocking collectives: 61.9 us -> none  [the longest x1 31.8 us: shards(): pooled_every = lax.all_gather(pooled, 'seq', axis=0, tiled=True)]
    pallas_call x0 -> x1, Pallas kernels: none -> 46.7 us  [shards(): pl.pallas_call(functools.partial(kernel, nz, nx, ny), out_shape=jax.Shape...]
    unnamed x8 -> x9, local copies, waits for them, and re-layouts: 18.2 us -> 4.37 us
    dot_general x6 -> x0, matrix products: 11.1 us -> none  [the longest x1 6.62 us: shards(): jnp.dot(normed, proj_weight, preferred_element_type=jnp.float32)]
    all_to_all x1 -> x0, blocking collectives: 10.9 us -> none  [shards(): lax.all_to_all(attended, 'seq', split_axis=0, concat_axis=1, tiled=True)]
    ppermute x1 -> x0, starting transfers between devices: 1.29 us -> none  [shifted(): return lax.ppermute(shard, axis, pairs)]
  transfers between devices with their start and end apart: 2 -> 0, of which waited for: 0 -> 0; matrix products, arithmetic and copies ran while one was open for 17% -> 0% of each run, Pallas kernels for 0% -> 0%
where the time goes in v1:
time: 52.6 us; the launch traced here: 52.4 us
  Pallas kernels  46.7 us (89%)
  local copies, waits for them, and re-layouts  5.05 us (10%)
  between operations  0.67 us (1%)
    pallas_call x1, Pallas kernels, shards(): pl.pallas_call(functools.partial(kernel, nz, nx, ny), out_shape=jax.Shape...  46.7 us
    unnamed x9, local copies, waits for them, and re-layouts  4.37 us

profile of v1, /device:TPU:0, one launch (start us, length us, event | category | flops | bytes accessed | tf_op | source)
XLA Modules:
  0.0 52.4 jit_solution(9393422963739862467)
XLA Ops:
  0.7 0.7 %reshape.14.gain = bf16[1,512]{1,0:T(2,128)(2,1)S(1)} reshape(bf16[512]{0:T(512)(128)(2,1)} %param.12) | data formatting | bytes 2048 | tf_op jit(solution)/shard_map/reshape | solution.py:295
  1.3 0.0 copy-start
  1.3 1.0 %copy-done = bf16[512,512]{1,0:T(8,128)(2,1)S(1)} copy-done((bf16[512,512]{1,0:T(8,128)(2,1)S(1)}, bf16[512,512]{1,0:T(8,128)(2,1)}, u32[]{:S(2)}) %copy-start) | copy-done | bytes 524312
  2.4 0.0 copy-start.1
  2.4 1.0 %copy-done.1 = bf16[512,512]{1,0:T(8,128)(2,1)S(1)} copy-done((bf16[512,512]{1,0:T(8,128)(2,1)S(1)}, bf16[512,512]{1,0:T(8,128)(2,1)}, u32[]{:S(2)}) %copy-start.1) | copy-done | bytes 524312
  3.4 0.0 copy-start.2
  3.4 0.9 %copy-done.2 = bf16[192,512]{1,0:T(8,128)(2,1)S(1)} copy-done((bf16[192,512]{1,0:T(8,128)(2,1)S(1)}, bf16[192,512]{1,0:T(8,128)(2,1)}, u32[]{:S(2)}) %copy-start.2) | copy-done | bytes 196632
  4.3 0.0 copy-start.3
  4.3 0.7 %copy-done.3 = s32[32]{0:T(128)S(1)} copy-done((s32[32]{0:T(128)S(1)}, s32[32]{0:T(128)}, u32[]{:S(2)}) %copy-start.3) | copy-done | bytes 152
  5.0 46.7 %shard_map.73 = bf16[32,4096]{1,0:T(8,128)(2,1)S(1)} custom-call(bf16[192,512]{1,0:T(8,128)(2,1)S(1)} %copy-done.2, s32[1,32]{1,0:T(1,128)S(1)} %bitcast.6, s32[1]{0:T(128)S(6)} %copy.9.straddle, bf16[512,512]{1,0:T(8,128)(2,1)S(1)} %copy-done, bf16[4,128,512]{2,1,0:T(8,128)(2,1)S(1)} %bitcast.5, bf16[1,512]{1,0:T(2,128)(2,1)S(1)} %reshape.14.gain, ...), custom_call_target="tpu_custom_call" | custom-call | flops 4294967296 | bytes 12582912 | tf_op jit(solution)/shard_map/pallas_call | solution.py:269
  51.7 0.7 %copy.10 = bf16[32,4096]{1,0:T(8,128)(2,1)} copy(bf16[32,4096]{1,0:T(8,128)(2,1)S(1)} %shard_map.73) | data formatting | bytes 524288
Async XLA Ops:
  1.3 1.0 %copy-start = (bf16[512,512]{1,0:T(8,128)(2,1)S(1)}, bf16[512,512]{1,0:T(8,128)(2,1)}, u32[]{:S(2)}) copy-start(bf16[512,512]{1,0:T(8,128)(2,1)} %key_weight.1) | copy-start | bytes 1572868
  2.4 1.0 %copy-start.1 = (bf16[512,512]{1,0:T(8,128)(2,1)S(1)}, bf16[512,512]{1,0:T(8,128)(2,1)}, u32[]{:S(2)}) copy-start(bf16[512,512]{1,0:T(8,128)(2,1)} %param.11) | copy-start | bytes 1572868
  3.4 0.9 %copy-start.2 = (bf16[192,512]{1,0:T(8,128)(2,1)S(1)}, bf16[192,512]{1,0:T(8,128)(2,1)}, u32[]{:S(2)}) copy-start(bf16[192,512]{1,0:T(8,128)(2,1)} %states.1) | copy-start | bytes 589828
  4.3 0.7 %copy-start.3 = (s32[32]{0:T(128)S(1)}, s32[32]{0:T(128)}, u32[]{:S(2)}) copy-start(s32[32]{0:T(128)} %param.8) | copy-start | bytes 388

commit v2 on v1

--- a/solution.py
+++ b/solution.py
@@ -12,7 +12,6 @@
 LHD = 128
 HALO = 64
 CORES = 2
-PAD = 16
 
 epsilon = 1e-05
 
@@ -40,10 +39,10 @@
     nz, nx, ny,
     states, starts, straddle, key_weight, out_weight, gain, attn_weight,
     out,
-    window, kw, ow, w, pg, acc, att,
+    window, kw, ow, w, pg, gv, gs, st, acc, att,
     l_sem, w_sem, h_sem,
     zs_sem, xs_sem, m_sem, ys_sem, yr_sem, cs_sem, cr_sem,
-    ps_sem, pr_sem, as_sem, ar_sem,
+    ps_sem, pr_sem, gs_sem, gr_sem, as_sem, ar_sem,
 ):
     n = nz * nx
     s = lax.axis_index("seq")
@@ -52,16 +51,27 @@
     yi, ci = r // CORES, r % CORES
     other = yi * CORES + (1 - ci)
     rows, width = states.shape
-    patches = starts.shape[1]
-    cols = out_weight.shape[2]
+    patches = starts.shape[0]
+    cols = out_weight.shape[3]
     heads = cols // HD
     model = cols * n
 
+    def flip(index, mask):
+        bit = 1
+        for _ in range(mask.bit_length()):
+            if mask & bit:
+                index = index + (1 - 2 * ((index // bit) % 2)) * bit
+            bit *= 2
+        return index
+
     def seq_of(kz, kx):
-        return ((zi + nz + kz) % nz) * nx + (xi + nx + kx) % nx
+        return flip(zi, kz) * nx + (xi + nx + kx) % nx
+
+    def y_of(ky):
+        return (yi + ny + ky) % ny
 
     def rep_of(ky):
-        return ((yi + ny + ky) % ny) * CORES + ci
+        return y_of(ky) * CORES + ci
 
     def remote(src, dst, send, recv, seq, rep):
         return pltpu.make_async_remote_copy(
@@ -85,13 +95,17 @@
 
     local = [
         pltpu.make_async_copy(states, window.at[pl.ds(0, rows)], l_sem.at[0]),
-        pltpu.make_async_copy(key_weight, kw, l_sem.at[1]),
-        pltpu.make_async_copy(out_weight, ow.at[s], l_sem.at[2]),
+        pltpu.make_async_copy(starts, st, l_sem.at[1]),
+        pltpu.make_async_copy(gain, gv, l_sem.at[2]),
+        pltpu.make_async_copy(key_weight, kw, l_sem.at[3]),
+        pltpu.make_async_copy(out_weight, ow.at[s], l_sem.at[4]),
     ]
     for copy in local:
         copy.start()
     w_copy = pltpu.make_async_copy(attn_weight, w, w_sem)
     w_copy.start()
+    local[2].wait()
+    gs[s] = gv[...].astype(F32).reshape(1, cols)
 
     pl.semaphore_wait(barrier, n - 1 + ny - 1 + 1)
 
@@ -111,11 +125,20 @@
         copy.start()
         sent.append(copy)
 
-    mine = out_weight.at[r]
+    full = [(0, kx) for kx in range(1, nx)] + ([(1, 0)] if nz > 1 else [])
+    z_order = list(range(2, nz)) + ([1] if nz > 1 else [])
+
+    def block(ref, j, o):
+        return ref.at[j, ci] if o in full else ref.at[j, ci, yi]
+
+    for kz in z_order:
+        o = (kz, 0)
+        source = out_weight.at[ci] if o in full else out_weight.at[ci, yi]
+        go(remote(source, block(ow, s, o), zs_sem.at[kz], m_sem.at[kz, 0], seq_of(kz, 0), r))
     for kx in range(1, nx):
-        go(remote(mine, ow.at[s, r], xs_sem.at[0, kx], m_sem.at[0, kx], seq_of(0, kx), r))
-    for kz in range(1, nz):
-        go(remote(mine, ow.at[s, r], zs_sem.at[kz], m_sem.at[kz, 0], seq_of(kz, 0), r))
+        go(remote(out_weight.at[ci], ow.at[s, ci], xs_sem.at[0, kx], m_sem.at[0, kx], seq_of(0, kx), r))
+    for k in range(1, n):
+        go(remote(gs.at[s], gs.at[s], gs_sem.at[k], gr_sem.at[k], (s + k) % n, r))
 
     @pl.when(s == n - 1)
     def _():
@@ -123,7 +146,8 @@
 
     square0 = lax.broadcasted_iota(jnp.int32, (patches, patches), 0)
     square1 = lax.broadcasted_iota(jnp.int32, (patches, patches), 1)
-    first = (starts[...] - s * rows).astype(F32)
+    local[1].wait()
+    first = (st[...].reshape(1, patches) - s * rows).astype(F32)
     low = jnp.sum(jnp.where(square0 == square1, first, 0.0), axis=1, keepdims=True)
     high = jnp.sum(jnp.where(square0 + 1 == square1, first, 0.0), axis=1, keepdims=True)
     line = lax.broadcasted_iota(jnp.int32, (patches, 1), 0)
@@ -133,7 +157,7 @@
     count = high - low
 
     local[0].wait()
-    local[1].wait()
+    local[3].wait()
 
     @pl.when(s < n - 1)
     def _():
@@ -145,40 +169,72 @@
     scale = F32(1.0 / math.sqrt(LHD))
     for h in range(width // LHD):
         part = slice(h * LHD, (h + 1) * LHD)
-        pg[s, pl.ds(0, patches), part] = softmax_dot(
+        pg[s, :, part] = softmax_dot(
             dot_t(query[:, part], keys[:, part]) * scale, member, whole[:, part]
         )
-    pg[s, pl.ds(patches, PAD), pl.ds(0, cols)] = jnp.broadcast_to(gain[...], (PAD, cols))
-    for k in range(1, n):
-        go(remote(pg.at[s], pg.at[s], ps_sem.at[k], pr_sem.at[k], (s + k) % n, r))
+    for kz in z_order:
+        go(remote(pg.at[s], pg.at[s], ps_sem.at[kz, 0], pr_sem.at[kz, 0], seq_of(kz, 0), r))
+    for kx in range(1, nx):
+        go(remote(pg.at[s], pg.at[s], ps_sem.at[0, kx], pr_sem.at[0, kx], seq_of(0, kx), r))
 
     def wait_for(ref, sem):
         pltpu.make_async_copy(ref, ref, sem).wait()
 
-    order = [(kz, kx) for kx in range(nx) for kz in range(nz)][1:]
-    if nx > 1:
-        order = [(0, kx) for kx in range(1, nx)] + [o for o in order if o[0] > 0]
-    for kz, kx in order:
-        j = seq_of(-kz, -kx)
-        piece = ow.at[j, r]
-        wait_for(piece, m_sem.at[kz, kx])
-        for ky in range(1, ny):
-            go(remote(piece, piece, ys_sem.at[ky, kz, kx], yr_sem.at[ky, kz, kx], s, rep_of(ky)))
+    def pass_on(o):
+        kz, kx = o
+        j = seq_of(kz, -kx)
+        got = block(ow, j, o)
+        piece = ow.at[j, ci, yi]
+        wait_for(got, m_sem.at[kz, kx])
+        if o not in full:
+            for ky in range(1, ny):
+                go(remote(piece, piece, ys_sem.at[ky, kz, kx], yr_sem.at[ky, kz, kx], s, rep_of(ky)))
         if kx == 0:
             for k in range(1, nx):
                 go(remote(piece, piece, xs_sem.at[kz, k], m_sem.at[kz, k], seq_of(0, k), r))
-        go(remote(piece, piece, cs_sem.at[0, kz, kx], cr_sem.at[0, kz, kx], s, other))
-
+        go(remote(got, got, cs_sem.at[0, kz, kx], cr_sem.at[0, kz, kx], s, other))
+
+    def pass_y(o):
+        kz, kx = o
+        for ky in range(1, ny):
+            piece = ow.at[seq_of(kz, -kx), ci, y_of(-ky)]
+            wait_for(piece, yr_sem.at[ky, kz, kx])
+            go(remote(piece, piece, cs_sem.at[ky, kz, kx], cr_sem.at[ky, kz, kx], s, other))
+
+    def arrived(o):
+        kz, kx = o
+        j = seq_of(kz, -kx)
+        if o in full:
+            wait_for(ow.at[j, 1 - ci], cr_sem.at[0, kz, kx])
+        else:
+            for ky in range(ny):
+                wait_for(ow.at[j, 1 - ci, y_of(-ky)], cr_sem.at[ky, kz, kx])
+        return j
+
+    for kz in z_order:
+        if (kz, 0) in full:
+            continue
+        pass_on((kz, 0))
+    for kz in z_order:
+        j = seq_of(kz, 0)
+        wait_for(pg.at[j], pr_sem.at[kz, 0])
+        for kx in range(1, nx):
+            go(remote(pg.at[j], pg.at[j], ps_sem.at[kz, kx], pr_sem.at[kz, kx], seq_of(0, kx), r))
+    for o in full[::-1]:
+        pass_on(o)
+
+    for kz in range(nz):
+        for kx in range(1, nx):
+            wait_for(pg.at[s], pr_sem.at[kz, kx])
     for k in range(1, n):
-        wait_for(pg.at[s], pr_sem.at[k])
-    pooled = pg[:, pl.ds(0, patches), :].reshape(n * patches, width)
+        wait_for(gs.at[s], gr_sem.at[k])
+    pooled = pg[...].reshape(n * patches, width)
 
     def project(j, squares, fresh):
         weight = ow[j].reshape(width, cols)
         embed = dot(pooled, weight)
         squares = squares + jnp.sum(embed * embed, axis=1, keepdims=True)
-        row = pg[j, pl.ds(patches, PAD), pl.ds(0, cols)][0:1, :].astype(F32)
-        scaled = (embed * row).astype(BF16)
+        scaled = (embed * gs[j]).astype(BF16)
         for t in range(3):
             span = slice(t * cols, (t + 1) * cols)
             term = dot(scaled, w[t, j])
@@ -188,27 +244,34 @@
                 acc[:, span] = acc[:, span] + term
         return squares
 
-    def arrived(kz, kx):
-        j = seq_of(-kz, -kx)
-        for ky in range(ny):
-            wait_for(ow.at[j, other], cr_sem.at[ky, kz, kx])
-        return j
-
-    local[2].wait()
+    late = [(kz, kx) for kz in z_order for kx in range(1, nx)]
+    early = [(kz, 0) for kz in z_order if (kz, 0) not in full]
+    ready, waiting = list(full), early + late
+    steps = []
+    for i, o in enumerate(late):
+        steps.append((pass_on, o))
+        if i < len(early):
+            steps.append((pass_y, o := early[i]))
+        if ready:
+            steps.append((None, ready.pop(0)))
+        if i < len(early):
+            ready.append(o)
+            waiting.remove(o)
+    for o in waiting:
+        steps.append((pass_y, o))
+        if ready:
+            steps.append((None, ready.pop(0)))
+        ready.append(o)
+    steps += [(None, o) for o in ready]
+
+    local[4].wait()
     w_copy.wait()
     squares = project(s, jnp.zeros((n * patches, 1), F32), True)
-    before = None
-    for kz, kx in order:
-        j = seq_of(-kz, -kx)
-        for ky in range(1, ny):
-            piece = ow.at[j, rep_of(-ky)]
-            wait_for(piece, yr_sem.at[ky, kz, kx])
-            go(remote(piece, piece, cs_sem.at[ky, kz, kx], cr_sem.at[ky, kz, kx], s, other))
-        if before is not None:
-            squares = project(arrived(*before), squares, False)
-        before = (kz, kx)
-    if before is not None:
-        squares = project(arrived(*before), squares, False)
+    for act, o in steps:
+        if act is None:
+            squares = project(arrived(o), squares, False)
+        else:
+            act(o)
 
     total = n * patches
     rstd = lax.rsqrt(squares / F32(model) + epsilon)
@@ -262,37 +325,39 @@
     total = n * patches
     w = attn_weight.transpose(1, 0, 2).reshape(three, n, model // n, cols)
     any_space = pl.BlockSpec(memory_space=pl.ANY)
-    vmem = pl.BlockSpec(memory_space=pltpu.VMEM)
     smem = pl.BlockSpec(memory_space=pltpu.SMEM)
     dma = pltpu.SemaphoreType.DMA
     flops = 2 * total * (model * three * cols + width * model)
     return pl.pallas_call(
         functools.partial(kernel, nz, nx, ny),
         out_shape=jax.ShapeDtypeStruct((patches, model), BF16),
-        in_specs=[any_space, vmem, smem, any_space, any_space, vmem, any_space],
+        in_specs=[any_space, any_space, smem, any_space, any_space, any_space, any_space],
         out_specs=any_space,
         scratch_shapes=[
             pltpu.VMEM((rows + HALO, width), BF16),
             pltpu.VMEM(key_weight.shape, BF16),
-            pltpu.VMEM((n, reps, width // reps, cols), BF16),
+            pltpu.VMEM((n, CORES, ny, width // reps, cols), BF16),
             pltpu.VMEM(w.shape, BF16),
-            pltpu.VMEM((n, patches + PAD, width), BF16),
+            pltpu.VMEM((n, patches, width), BF16),
+            pltpu.VMEM((cols,), BF16),
+            pltpu.VMEM((n, 1, cols), F32),
+            pltpu.VMEM((patches,), jnp.int32),
             pltpu.VMEM((total, three * cols), F32),
             pltpu.VMEM((heads, n, patches, HD), BF16),
-            dma((3,)), dma, dma((2,)),
+            dma((5,)), dma, dma((2,)),
             dma((nz,)), dma((nz, nx)), dma((nz, nx)),
             dma((ny, nz, nx)), dma((ny, nz, nx)), dma((ny, nz, nx)), dma((ny, nz, nx)),
-            dma((n,)), dma((n,)), dma((heads, n)), dma((heads, n)),
+            dma((nz, nx)), dma((nz, nx)), dma((n,)), dma((n,)), dma((heads, n)), dma((heads, n)),
         ],
         compiler_params=pltpu.CompilerParams(
-            collective_id=0, has_side_effects=True, vmem_limit_bytes=48 * 1024 * 1024
+            collective_id=0, has_side_effects=True, vmem_limit_bytes=60 * 1024 * 1024
         ),
         cost_estimate=pl.CostEstimate(
             flops=flops, bytes_accessed=w.size * 2, transcendentals=0
         ),
     )(
-        states, starts.reshape(1, patches), straddle, key_weight,
-        out_weight.reshape(reps, width // reps, cols), norm_gain.reshape(1, cols), w,
+        states, starts, straddle, key_weight,
+        out_weight.reshape(CORES, ny, width // reps, cols), norm_gain, w,
     )
 
 

time: 52.6 us -> 49.2 us (0.935)
  local copies, waits for them, and re-layouts: 5.05 us -> 1.67 us
    unnamed x9 -> x1, local copies, waits for them, and re-layouts: 4.37 us -> 1.67 us
    reshape x1 -> x0, local copies, waits for them, and re-layouts: 0.68 us -> none  [shards(): norm_gain.reshape(1, cols)]
where the time goes in v2:
time: 49.2 us; the launch traced here: 49.1 us
  Pallas kernels  46.7 us (95%)
  local copies, waits for them, and re-layouts  1.67 us (3%)
  between operations  0.66 us (1%)
    pallas_call x1, Pallas kernels, shards(): pl.pallas_call(functools.partial(kernel, nz, nx, ny), out_shape=jax.Shape...  46.7 us
    unnamed x1, local copies, waits for them, and re-layouts  1.67 us

profile of v2, /device:TPU:0, one launch (start us, length us, event | category | flops | bytes accessed | tf_op | source)
XLA Modules:
  0.0 49.1 jit_solution(13132370471044106356)
XLA Ops:
  0.7 46.7 %shard_map.73 = bf16[32,4096]{1,0:T(8,128)(2,1)} custom-call(bf16[192,512]{1,0:T(8,128)(2,1)} %states.1, s32[32]{0:T(128)} %starts.1, s32[1]{0:T(128)S(6)} %copy.9.straddle, bf16[512,512]{1,0:T(8,128)(2,1)} %key_weight.1, bf16[2,2,128,512]{3,2,1,0:T(8,128)(2,1)} %bitcast.5, bf16[512]{0:T(512)(128)(2,1)} %gain.1, bf16[3,8,512,512]{3,2,1,0:T(8,128)(2,1)} %bitcast.4), custom_call_target="tpu_custom_call" | custom-call | flops 4294967296 | bytes 12582912 | tf_op jit(solution)/shard_map/pallas_call | solution.py:331
  47.4 1.7 %copy.10 = bf16[32,4096]{1,0:T(8,128)(2,1)} copy(bf16[32,4096]{1,0:T(8,128)(2,1)} %shard_map.73) | data formatting | bytes 524288

commit v3 on v2

--- a/solution.py
+++ b/solution.py
@@ -41,7 +41,7 @@
     out,
     window, kw, ow, w, pg, gv, gs, st, acc, att,
     l_sem, w_sem, h_sem,
-    zs_sem, xs_sem, m_sem, ys_sem, yr_sem, cs_sem, cr_sem,
+    zs_sem, zr_sem, xs_sem, xr_sem, es_sem, er_sem, ys_sem, yr_sem, cs_sem, cr_sem,
     ps_sem, pr_sem, gs_sem, gr_sem, as_sem, ar_sem,
 ):
     n = nz * nx
@@ -119,24 +119,87 @@
     def _():
         halo.start()
 
-    sent = []
+    sent, maybe = [], []
 
     def go(copy):
         copy.start()
         sent.append(copy)
 
-    full = [(0, kx) for kx in range(1, nx)] + ([(1, 0)] if nz > 1 else [])
-    z_order = list(range(2, nz)) + ([1] if nz > 1 else [])
-
-    def block(ref, j, o):
-        return ref.at[j, ci] if o in full else ref.at[j, ci, yi]
-
-    for kz in z_order:
-        o = (kz, 0)
-        source = out_weight.at[ci] if o in full else out_weight.at[ci, yi]
-        go(remote(source, block(ow, s, o), zs_sem.at[kz], m_sem.at[kz, 0], seq_of(kz, 0), r))
-    for kx in range(1, nx):
-        go(remote(out_weight.at[ci], ow.at[s, ci], xs_sem.at[0, kx], m_sem.at[0, kx], seq_of(0, kx), r))
+    def go_if(cond, copy):
+        @pl.when(cond)
+        def _():
+            copy.start()
+
+        maybe.append((cond, copy))
+
+    even = 1 - zi % 2
+    short = jnp.minimum(zi, nz - 1 - zi)
+
+    def near(t):
+        if t == 0:
+            return zi
+        ahead = even if t % 2 == 1 else 1 - even
+        both = zi + (2 * ahead - 1) * ((t + 1) // 2)
+        lone = jnp.where(zi * 2 < nz, zi + t - short, zi - t + short)
+        return jnp.where(t <= 2 * short, both, lone)
+
+    line_z = [near(t) for t in range(nz)]
+
+    def shard_of(o):
+        return line_z[o[0]] * nx + (xi + nx - o[1]) % nx
+
+    def wait_for(ref, sem):
+        pltpu.make_async_copy(ref, ref, sem).wait()
+
+    whole_ones = [(0, kx) for kx in range(1, nx)] + ([(1, 0)] if nz > 1 else [])
+
+    mine = out_weight.at[ci, yi]
+    for side in range(2):
+        z_to = zi + 2 * side - 1
+        go_if(
+            (z_to >= 0) & (z_to < nz),
+            remote(mine, ow.at[s, ci, yi], zs_sem.at[0, side], zr_sem.at[zi], z_to * nx + xi, r),
+        )
+    for k in range(1, nx):
+        go(remote(mine, ow.at[s, ci, yi], xs_sem.at[0, k], xr_sem.at[0, k], seq_of(0, k), r))
+
+    def send_rest(k, seq):
+        for ky in range(1, ny):
+            part = y_of(-ky)
+            go(remote(out_weight.at[ci, part], ow.at[s, ci, part], es_sem.at[k, ky], er_sem.at[k, ky], seq, r))
+
+    def pass_first(o):
+        t, kx = o
+        j = shard_of(o)
+        piece = ow.at[j, ci, yi]
+        wait_for(piece, zr_sem.at[line_z[t]] if kx == 0 else xr_sem.at[t, kx])
+        if kx == 0:
+            z_to = jnp.where(line_z[t] < zi, zi + 1, zi - 1)
+            go_if(
+                (z_to >= 0) & (z_to < nz),
+                remote(piece, piece, zs_sem.at[t, 0], zr_sem.at[line_z[t]], z_to * nx + xi, r),
+            )
+            for k in range(1, nx):
+                go(remote(piece, piece, xs_sem.at[t, k], xr_sem.at[t, k], seq_of(0, k), r))
+        if o not in whole_ones:
+            for ky in range(1, ny):
+                go(remote(piece, piece, ys_sem.at[ky, t, kx], yr_sem.at[ky, t, kx], s, rep_of(ky)))
+        go(remote(piece, piece, cs_sem.at[0, t, kx], cr_sem.at[0, t, kx], s, other))
+
+    def pass_rest(o):
+        t, kx = o
+        for ky in range(1, ny):
+            piece = ow.at[shard_of(o), ci, y_of(-ky)]
+            wait_for(piece, er_sem.at[kx, ky] if o in whole_ones else yr_sem.at[ky, t, kx])
+            go(remote(piece, piece, cs_sem.at[ky, t, kx], cr_sem.at[ky, t, kx], s, other))
+
+    def arrived(o):
+        t, kx = o
+        j = shard_of(o)
+        for ky in range(ny):
+            wait_for(ow.at[j, 1 - ci, y_of(-ky)], cr_sem.at[ky, t, kx])
+        return j
+
     for k in range(1, n):
         go(remote(gs.at[s], gs.at[s], gs_sem.at[k], gr_sem.at[k], (s + k) % n, r))
 
@@ -163,6 +226,13 @@
     def _():
         halo.wait_recv()
 
+    for t in range(1, min(nz, 3)):
+        pass_first((t, 0))
+        if t == 1:
+            send_rest(0, flip(zi, 1) * nx + xi)
+    for k in range(1, nx):
+        send_rest(k, seq_of(0, k))
+
     whole = window[...]
     keys = dot(whole, kw[...]).astype(BF16)
     query = (dot(member.astype(BF16), whole) / count).astype(BF16)
@@ -172,56 +242,25 @@
         pg[s, :, part] = softmax_dot(
             dot_t(query[:, part], keys[:, part]) * scale, member, whole[:, part]
         )
-    for kz in z_order:
+    for kz in range(1, nz):
         go(remote(pg.at[s], pg.at[s], ps_sem.at[kz, 0], pr_sem.at[kz, 0], seq_of(kz, 0), r))
     for kx in range(1, nx):
         go(remote(pg.at[s], pg.at[s], ps_sem.at[0, kx], pr_sem.at[0, kx], seq_of(0, kx), r))
 
-    def wait_for(ref, sem):
-        pltpu.make_async_copy(ref, ref, sem).wait()
-
-    def pass_on(o):
-        kz, kx = o
-        j = seq_of(kz, -kx)
-        got = block(ow, j, o)
-        piece = ow.at[j, ci, yi]
-        wait_for(got, m_sem.at[kz, kx])
-        if o not in full:
-            for ky in range(1, ny):
-                go(remote(piece, piece, ys_sem.at[ky, kz, kx], yr_sem.at[ky, kz, kx], s, rep_of(ky)))
-        if kx == 0:
-            for k in range(1, nx):
-                go(remote(piece, piece, xs_sem.at[kz, k], m_sem.at[kz, k], seq_of(0, k), r))
-        go(remote(got, got, cs_sem.at[0, kz, kx], cr_sem.at[0, kz, kx], s, other))
-
-    def pass_y(o):
-        kz, kx = o
-        for ky in range(1, ny):
-            piece = ow.at[seq_of(kz, -kx), ci, y_of(-ky)]
-            wait_for(piece, yr_sem.at[ky, kz, kx])
-            go(remote(piece, piece, cs_sem.at[ky, kz, kx], cr_sem.at[ky, kz, kx], s, other))
-
-    def arrived(o):
-        kz, kx = o
-        j = seq_of(kz, -kx)
-        if o in full:
-            wait_for(ow.at[j, 1 - ci], cr_sem.at[0, kz, kx])
-        else:
-            for ky in range(ny):
-                wait_for(ow.at[j, 1 - ci, y_of(-ky)], cr_sem.at[ky, kz, kx])
-        return j
-
-    for kz in z_order:
-        if (kz, 0) in full:
-            continue
-        pass_on((kz, 0))
-    for kz in z_order:
+    for k in range(1, nx):
+        pass_first((0, k))
+    for t in range(3, nz):
+        pass_first((t, 0))
+    late = [(t, kx) for t in range(1, nz) for kx in range(1, nx)]
+    for o in late[:1]:
+        pass_first(o)
+    for kz in range(1, nz):
         j = seq_of(kz, 0)
         wait_for(pg.at[j], pr_sem.at[kz, 0])
         for kx in range(1, nx):
             go(remote(pg.at[j], pg.at[j], ps_sem.at[kz, kx], pr_sem.at[kz, kx], seq_of(0, kx), r))
-    for o in full[::-1]:
-        pass_on(o)
+    for o in late[1:2]:
+        pass_first(o)
 
     for kz in range(nz):
         for kx in range(1, nx):
@@ -244,22 +283,14 @@
                 acc[:, span] = acc[:, span] + term
         return squares
 
-    late = [(kz, kx) for kz in z_order for kx in range(1, nx)]
-    early = [(kz, 0) for kz in z_order if (kz, 0) not in full]
-    ready, waiting = list(full), early + late
-    steps = []
-    for i, o in enumerate(late):
-        steps.append((pass_on, o))
-        if i < len(early):
-            steps.append((pass_y, o := early[i]))
-        if ready:
-            steps.append((None, ready.pop(0)))
-        if i < len(early):
-            ready.append(o)
-            waiting.remove(o)
-    for o in waiting:
-        steps.append((pass_y, o))
-        if ready:
+    rest = [(1, 0)] if nz > 1 else []
+    rest += [(0, kx) for kx in range(1, nx)] + [(t, 0) for t in range(2, nz)] + late
+    still, ready, steps = late[2:], [], []
+    for i, o in enumerate(rest):
+        steps.append((pass_rest, o))
+        if i < len(still):
+            steps.append((pass_first, still[i]))
+        if i >= 2:
             steps.append((None, ready.pop(0)))
         ready.append(o)
     steps += [(None, o) for o in ready]
@@ -301,6 +332,8 @@
             wait_for(out.at[:, span], ar_sem.at[h, k])
     for copy in sent:
         copy.wait_send()
+    for cond, copy in maybe:
+        pl.when(cond)(copy.wait_send)
 
     @pl.when(s > 0)
     def _():
@@ -332,7 +365,7 @@
         functools.partial(kernel, nz, nx, ny),
         out_shape=jax.ShapeDtypeStruct((patches, model), BF16),
         in_specs=[any_space, any_space, smem, any_space, any_space, any_space, any_space],
-        out_specs=any_space,
+        out_specs=pl.BlockSpec(memory_space=pltpu.VMEM),
         scratch_shapes=[
             pltpu.VMEM((rows + HALO, width), BF16),
             pltpu.VMEM(key_weight.shape, BF16),
@@ -345,7 +378,7 @@
             pltpu.VMEM((total, three * cols), F32),
             pltpu.VMEM((heads, n, patches, HD), BF16),
             dma((5,)), dma, dma((2,)),
-            dma((nz,)), dma((nz, nx)), dma((nz, nx)),
+            dma((nz, 2)), dma((nz,)), dma((nz, nx)), dma((nz, nx)), dma((nx, ny)), dma((nx, ny)),
             dma((ny, nz, nx)), dma((ny, nz, nx)), dma((ny, nz, nx)), dma((ny, nz, nx)),
             dma((nz, nx)), dma((nz, nx)), dma((n,)), dma((n,)), dma((heads, n)), dma((heads, n)),
         ],

time: 49.2 us -> 49.4 us (level)
  no operation moved by 1% of the time
where the time goes in v3:
time: 49.4 us; the launch traced here: 49.3 us
  Pallas kernels  46.9 us (95%)
  local copies, waits for them, and re-layouts  1.67 us (3%)
  between operations  0.66 us (1%)
    pallas_call x1, Pallas kernels, shards(): pl.pallas_call(functools.partial(kernel, nz, nx, ny), out_shape=jax.Shape...  46.9 us
    unnamed x1, local copies, waits for them, and re-layouts  1.67 us

profile of v3, /device:TPU:0, one launch (start us, length us, event | category | flops | bytes accessed | tf_op | source)
XLA Modules:
  0.0 49.3 jit_solution(9747578055492157075)
XLA Ops:
  0.7 46.9 %shard_map.73 = bf16[32,4096]{1,0:T(8,128)(2,1)} custom-call(bf16[192,512]{1,0:T(8,128)(2,1)} %states.1, s32[32]{0:T(128)} %starts.1, s32[1]{0:T(128)S(6)} %copy.9.straddle, bf16[512,512]{1,0:T(8,128)(2,1)} %key_weight.1, bf16[2,2,128,512]{3,2,1,0:T(8,128)(2,1)} %bitcast.5, bf16[512]{0:T(512)(128)(2,1)} %gain.1, bf16[3,8,512,512]{3,2,1,0:T(8,128)(2,1)} %bitcast.4), custom_call_target="tpu_custom_call" | custom-call | flops 4294967296 | bytes 12582912 | tf_op jit(solution)/shard_map/pallas_call | solution.py:364
  47.6 1.7 %copy.10 = bf16[32,4096]{1,0:T(8,128)(2,1)} copy(bf16[32,4096]{1,0:T(8,128)(2,1)} %shard_map.73) | data formatting | bytes 524288

commit v4 on v3

--- a/solution.py
+++ b/solution.py
@@ -12,6 +12,7 @@
 LHD = 128
 HALO = 64
 CORES = 2
+CHUNKS = 2
 
 epsilon = 1e-05
 
@@ -52,7 +53,7 @@
     other = yi * CORES + (1 - ci)
     rows, width = states.shape
     patches = starts.shape[0]
-    cols = out_weight.shape[3]
+    cols = out_weight.shape[4]
     heads = cols // HD
     model = cols * n
 
@@ -153,51 +154,63 @@
 
     whole_ones = [(0, kx) for kx in range(1, nx)] + ([(1, 0)] if nz > 1 else [])
 
-    mine = out_weight.at[ci, yi]
-    for side in range(2):
-        z_to = zi + 2 * side - 1
-        go_if(
-            (z_to >= 0) & (z_to < nz),
-            remote(mine, ow.at[s, ci, yi], zs_sem.at[0, side], zr_sem.at[zi], z_to * nx + xi, r),
-        )
-    for k in range(1, nx):
-        go(remote(mine, ow.at[s, ci, yi], xs_sem.at[0, k], xr_sem.at[0, k], seq_of(0, k), r))
+    for c in range(CHUNKS):
+        mine = out_weight.at[ci, yi, c]
+        here = ow.at[s, ci, yi, c]
+        for side in range(2):
+            z_to = zi + 2 * side - 1
+            go_if(
+                (z_to >= 0) & (z_to < nz),
+                remote(mine, here, zs_sem.at[0, side, c], zr_sem.at[zi, c], z_to * nx + xi, r),
+            )
+        for k in range(1, nx):
+            go(remote(mine, here, xs_sem.at[0, k, c], xr_sem.at[0, k, c], seq_of(0, k), r))
 
     def send_rest(k, seq):
         for ky in range(1, ny):
             part = y_of(-ky)
-            go(remote(out_weight.at[ci, part], ow.at[s, ci, part], es_sem.at[k, ky], er_sem.at[k, ky], seq, r))
+            for c in range(CHUNKS):
+                go(remote(
+                    out_weight.at[ci, part, c], ow.at[s, ci, part, c],
+                    es_sem.at[k, ky, c], er_sem.at[k, ky, c], seq, r,
+                ))
 
     def pass_first(o):
+        for c in range(CHUNKS):
+            pass_chunk(o, c)
+
+    def pass_chunk(o, c):
         t, kx = o
         j = shard_of(o)
-        piece = ow.at[j, ci, yi]
-        wait_for(piece, zr_sem.at[line_z[t]] if kx == 0 else xr_sem.at[t, kx])
+        piece = ow.at[j, ci, yi, c]
+        wait_for(piece, zr_sem.at[line_z[t], c] if kx == 0 else xr_sem.at[t, kx, c])
         if kx == 0:
             z_to = jnp.where(line_z[t] < zi, zi + 1, zi - 1)
             go_if(
                 (z_to >= 0) & (z_to < nz),
-                remote(piece, piece, zs_sem.at[t, 0], zr_sem.at[line_z[t]], z_to * nx + xi, r),
+                remote(piece, piece, zs_sem.at[t, 0, c], zr_sem.at[line_z[t], c], z_to * nx + xi, r),
             )
             for k in range(1, nx):
-                go(remote(piece, piece, xs_sem.at[t, k], xr_sem.at[t, k], seq_of(0, k), r))
+                go(remote(piece, piece, xs_sem.at[t, k, c], xr_sem.at[t, k, c], seq_of(0, k), r))
         if o not in whole_ones:
             for ky in range(1, ny):
-                go(remote(piece, piece, ys_sem.at[ky, t, kx], yr_sem.at[ky, t, kx], s, rep_of(ky)))
-        go(remote(piece, piece, cs_sem.at[0, t, kx], cr_sem.at[0, t, kx], s, other))
+                go(remote(piece, piece, ys_sem.at[ky, t, kx, c], yr_sem.at[ky, t, kx, c], s, rep_of(ky)))
+        go(remote(piece, piece, cs_sem.at[0, t, kx, c], cr_sem.at[0, t, kx, c], s, other))
 
     def pass_rest(o):
         t, kx = o
         for ky in range(1, ny):
-            piece = ow.at[shard_of(o), ci, y_of(-ky)]
-            wait_for(piece, er_sem.at[kx, ky] if o in whole_ones else yr_sem.at[ky, t, kx])
-            go(remote(piece, piece, cs_sem.at[ky, t, kx], cr_sem.at[ky, t, kx], s, other))
+            for c in range(CHUNKS):
+                piece = ow.at[shard_of(o), ci, y_of(-ky), c]
+                wait_for(piece, er_sem.at[kx, ky, c] if o in whole_ones else yr_sem.at[ky, t, kx, c])
+                go(remote(piece, piece, cs_sem.at[ky, t, kx, c], cr_sem.at[ky, t, kx, c], s, other))
 
     def arrived(o):
         t, kx = o
         j = shard_of(o)
         for ky in range(ny):
-            wait_for(ow.at[j, 1 - ci, y_of(-ky)], cr_sem.at[ky, t, kx])
+            for c in range(CHUNKS):
+                wait_for(ow.at[j, 1 - ci, y_of(-ky), c], cr_sem.at[ky, t, kx, c])
         return j
 
     for k in range(1, n):
@@ -369,7 +382,7 @@
         scratch_shapes=[
             pltpu.VMEM((rows + HALO, width), BF16),
             pltpu.VMEM(key_weight.shape, BF16),
-            pltpu.VMEM((n, CORES, ny, width // reps, cols), BF16),
+            pltpu.VMEM((n, CORES, ny, CHUNKS, width // reps // CHUNKS, cols), BF16),
             pltpu.VMEM(w.shape, BF16),
             pltpu.VMEM((n, patches, width), BF16),
             pltpu.VMEM((cols,), BF16),
@@ -378,8 +391,9 @@
             pltpu.VMEM((total, three * cols), F32),
             pltpu.VMEM((heads, n, patches, HD), BF16),
             dma((5,)), dma, dma((2,)),
-            dma((nz, 2)), dma((nz,)), dma((nz, nx)), dma((nz, nx)), dma((nx, ny)), dma((nx, ny)),
-            dma((ny, nz, nx)), dma((ny, nz, nx)), dma((ny, nz, nx)), dma((ny, nz, nx)),
+            dma((nz, 2, CHUNKS)), dma((nz, CHUNKS)), dma((nz, nx, CHUNKS)), dma((nz, nx, CHUNKS)),
+            dma((nx, ny, CHUNKS)), dma((nx, ny, CHUNKS)),
+            *(dma((ny, nz, nx, CHUNKS)) for _ in range(4)),
             dma((nz, nx)), dma((nz, nx)), dma((n,)), dma((n,)), dma((heads, n)), dma((heads, n)),
         ],
         compiler_params=pltpu.CompilerParams(
@@ -390,7 +404,7 @@
         ),
     )(
         states, starts, straddle, key_weight,
-        out_weight.reshape(CORES, ny, width // reps, cols), norm_gain, w,
+        out_weight.reshape(CORES, ny, CHUNKS, width // reps // CHUNKS, cols), norm_gain, w,
     )
 
 

time: 49.4 us -> 50.4 us (1.020)
  Pallas kernels: 46.9 us -> 47.9 us
    pallas_call x1, Pallas kernels: 46.9 us -> 47.9 us  [shards(): pl.pallas_call(functools.partial(kernel, nz, nx, ny), out_shape=jax.Shape...]
where the time goes in v4:
time: 50.4 us; the launch traced here: 50.2 us
  Pallas kernels  47.9 us (95%)
  local copies, waits for them, and re-layouts  1.67 us (3%)
  between operations  0.66 us (1%)
    pallas_call x1, Pallas kernels, shards(): pl.pallas_call(functools.partial(kernel, nz, nx, ny), out_shape=jax.Shape...  47.9 us
    unnamed x1, local copies, waits for them, and re-layouts  1.67 us

profile of v4, /device:TPU:0, one launch (start us, length us, event | category | flops | bytes accessed | tf_op | source)
XLA Modules:
  0.0 50.2 jit_solution(16375374926961755008)
XLA Ops:
  0.7 47.9 %shard_map.73 = bf16[32,4096]{1,0:T(8,128)(2,1)} custom-call(bf16[192,512]{1,0:T(8,128)(2,1)} %states.1, s32[32]{0:T(128)} %starts.1, s32[1]{0:T(128)S(6)} %copy.9.straddle, bf16[512,512]{1,0:T(8,128)(2,1)} %key_weight.1, bf16[2,2,2,64,512]{4,3,2,1,0:T(8,128)(2,1)} %bitcast.5, bf16[512]{0:T(512)(128)(2,1)} %gain.1, bf16[3,8,512,512]{3,2,1,0:T(8,128)(2,1)} %bitcast.4), custom_call_target="tpu_custom_call" | custom-call | flops 4294967296 | bytes 12582912 | tf_op jit(solution)/shard_map/pallas_call | solution.py:377
  48.5 1.7 %copy.10 = bf16[32,4096]{1,0:T(8,128)(2,1)} copy(bf16[32,4096]{1,0:T(8,128)(2,1)} %shard_map.73) | data formatting | bytes 524288
